TPU v7x, 256 devices: a whole 4x4x8 slice. The times are simulated.
256 devices in a mesh: expert: 32 (over y, x, core), replica: 8 (over z).
Axes of the slice: x: 4, y: 4, z: 8, core: 2. Of those that a mesh axis runs over, the one named last changes fastest.
Arguments:
- tokens: bfloat16 [131072, 2048], P(('expert', 'replica')), may hold values from -6 to 6
- d_hidden: bfloat16 [131072, 768], P(('expert', 'replica')), may hold values from -6 to 6
- w_gate: bfloat16 [128, 2048, 768], P(None, ('expert', 'replica')), may hold values from -0.125 to 0.125
- w_up: bfloat16 [128, 2048, 768], P(None, ('expert', 'replica')), may hold values from -0.125 to 0.125
- expert_ids: int32 [256], replicated, may hold values from 0 to 127
Outputs:
- hidden: bfloat16 [131072, 768], P(('expert', 'replica'))
- token_grad: bfloat16 [131072, 2048], P(('expert', 'replica'))
- grad_gate: bfloat16 [128, 2048, 768], P(None, ('expert', 'replica'))
- grad_up: bfloat16 [128, 2048, 768], P(None, ('expert', 'replica'))
Inputs may be any that keep to these rules, and one draw needn't show every extreme that they name: expert_ids[b] is the expert used by the rows of block b; several blocks may use the same expert.
All inputs are finite; a program needn't handle non-finite values.
Results may differ from a plain program's by a relative error of at most 0.0057.
Values may be sent and summed in bfloat16 or wider, within the bound.
No kernel may reach another device: no remote copies, remote signals or barrier semaphores. Data moves between devices by JAX's collectives and lax.ppermute only.
A program may use at most 128 MiB of HBM per device.

v0:
```python
import jax
import jax.numpy as jnp
from jax import lax
from jax.sharding import PartitionSpec as P


def pick_pieces(weights, chosen, leading):
    return jnp.take(weights, chosen, axis=0).reshape(leading + weights.shape[1:])


def per_device(tokens, d_hidden, w_gate, w_up, expert_ids):
    owner_count = lax.axis_size("expert")
    member_count = lax.axis_size("replica")
    block_rows = w_gate.shape[1]
    hidden_width = w_gate.shape[2]
    model_width = owner_count * member_count * block_rows
    leading = (owner_count, member_count)
    outgoing = (pick_pieces(w_gate, expert_ids, leading), pick_pieces(w_up, expert_ids, leading))
    gate_parts, up_parts = (
        lax.all_to_all(
            lax.all_to_all(outgoing[0], "expert", split_axis=0, concat_axis=0, tiled=True),
            "replica",
            split_axis=1,
            concat_axis=1,
            tiled=True,
        ),
        lax.all_to_all(
            lax.all_to_all(outgoing[1], "expert", split_axis=0, concat_axis=0, tiled=True),
            "replica",
            split_axis=1,
            concat_axis=1,
            tiled=True,
        ),
    )
    gate_whole = gate_parts.reshape(model_width, hidden_width)
    up_whole = up_parts.reshape(model_width, hidden_width)
    gate_pre = jnp.dot(tokens, gate_whole, preferred_element_type=jnp.float32)
    up_pre = jnp.dot(tokens, up_whole, preferred_element_type=jnp.float32)
    sigmoid_gate = jax.nn.sigmoid(gate_pre)
    activated = gate_pre * sigmoid_gate
    hidden = (activated * up_pre).astype(jnp.bfloat16)
    upstream = d_hidden.astype(jnp.float32)
    d_gate = (upstream * up_pre * sigmoid_gate * (1.0 + gate_pre * (1.0 - sigmoid_gate))).astype(
        jnp.bfloat16
    )
    d_up = (upstream * activated).astype(jnp.bfloat16)
    back_dims = (((1,), (1,)), ((), ()))
    token_grad = (
        lax.dot_general(d_gate, gate_whole, back_dims, preferred_element_type=jnp.float32)
        + lax.dot_general(d_up, up_whole, back_dims, preferred_element_type=jnp.float32)
    ).astype(jnp.bfloat16)
    outer_dims = (((0,), (0,)), ((), ()))
    shape_parts = (owner_count, member_count, block_rows, hidden_width)
    part_gate = (
        lax.dot_general(tokens, d_gate, outer_dims, preferred_element_type=jnp.float32)
        .astype(jnp.bfloat16)
        .reshape(shape_parts)
    )
    part_up = (
        lax.dot_general(tokens, d_up, outer_dims, preferred_element_type=jnp.float32)
        .astype(jnp.bfloat16)
        .reshape(shape_parts)
    )
    gate_terms, up_terms = (
        lax.all_to_all(
            lax.all_to_all(part_gate, "replica", split_axis=1, concat_axis=1, tiled=True),
            "expert",
            split_axis=0,
            concat_axis=0,
            tiled=True,
        ),
        lax.all_to_all(
            lax.all_to_all(part_up, "replica", split_axis=1, concat_axis=1, tiled=True),
            "expert",
            split_axis=0,
            concat_axis=0,
            tiled=True,
        ),
    )
    block_count = owner_count * member_count
    expert_total = w_gate.shape[0]
    selector = (expert_ids[None, :] == jnp.arange(expert_total, dtype=jnp.int32)[:, None]).astype(
        jnp.bfloat16
    )
    scale = tokens.shape[0] ** (-0.5)
    flat_gate = gate_terms.reshape(block_count, block_rows * hidden_width)
    flat_up = up_terms.reshape(block_count, block_rows * hidden_width)
    grad_gate = (
        (jnp.dot(selector, flat_gate, preferred_element_type=jnp.float32) * scale)
        .reshape(expert_total, block_rows, hidden_width)
        .astype(jnp.bfloat16)
    )
    grad_up = (
        (jnp.dot(selector, flat_up, preferred_element_type=jnp.float32) * scale)
        .reshape(expert_total, block_rows, hidden_width)
        .astype(jnp.bfloat16)
    )
    return (hidden, token_grad, grad_gate, grad_up)


def solution(mesh):
    in_specs = (
        P(("expert", "replica"), None),
        P(("expert", "replica"), None),
        P(None, ("expert", "replica"), None),
        P(None, ("expert", "replica"), None),
        P(),
    )
    out_specs = (
        P(("expert", "replica"), None),
        P(("expert", "replica"), None),
        P(None, ("expert", "replica"), None),
        P(None, ("expert", "replica"), None),
    )
    return jax.shard_map(
        per_device, mesh=mesh, in_specs=in_specs, out_specs=out_specs, check_vma=False
    )
```

profile of v0, /device:TPU:1, one launch (start us, length us, event | category | flops | bytes accessed | tf_op | source)
XLA Modules:
  0.0 514.6 jit_solution(12637816666306035517)
XLA Ops:
  0.6 0.0 copy-start
  0.6 0.8 compare_and_fusion
  1.5 0.7 compare_select_fusion
  2.2 3.8 gather_fusion.1
  6.0 3.8 gather_fusion
  9.8 4.5 broadcast_select_fusion.1
  14.4 48.1 %all_to_all.40 = bf16[32,8,8,768]{3,2,1,0:T(8,128)(2,1)} all-to-all(bf16[32,8,8,768]{3,2,1,0:T(8,128)(2,1)S(1)} %bitcast.66), channel_id=1, replica_groups=mesh['expert'=32,'replica'=8] {'expert'}, dimensions={0} | all-to-all | bytes 6291456 | tf_op jit(solution)/shard_map/all_to_all | solution.py:21
  62.5 4.8 all-to-all-start.2
  67.3 3.8 copy.35
  71.1 35.5 %all-to-all-done.2 = bf16[32,8,8,768]{3,2,1,0:T(8,128)(2,1)} async-done(((bf16[32,8,8,768]{3,2,1,0:T(8,128)(2,1)}), bf16[32,8,8,768]{3,2,1,0:T(8,128)(2,1)}, u32[]{:S(2)}, u32[]{:S(2)}) %all-to-all-start.2) | async-done | bytes 3145760 | tf_op jit(solution)/shard_map/all_to_all | solution.py:28
  106.6 8.2 %all-to-all-start.1 = ((bf16[32,8,8,768]{3,2,0,1:T(8,128)(2,1)}), bf16[32,8,8,768]{3,2,0,1:T(8,128)(2,1)}, u32[]{:S(2)}, u32[]{:S(2)}) async-start(bf16[32,8,8,768]{3,2,0,1:T(8,128)(2,1)} %copy.35), calls=%async_computation.1 | async-start | bytes 6291456 | tf_op jit(solution)/shard_map/all_to_all | solution.py:20
  114.8 3.8 copy.37
  118.6 70.4 %all-to-all-done.1 = bf16[32,8,8,768]{3,2,0,1:T(8,128)(2,1)} async-done(((bf16[32,8,8,768]{3,2,0,1:T(8,128)(2,1)}), bf16[32,8,8,768]{3,2,0,1:T(8,128)(2,1)}, u32[]{:S(2)}, u32[]{:S(2)}) %all-to-all-start.1) | async-done | bytes 3145760 | tf_op jit(solution)/shard_map/all_to_all | solution.py:20
  189.0 4.5 all-to-all-start.3
  193.5 1.2 copy.39
  194.6 2.3 copy.36
  196.9 0.0 copy-start.5
  196.9 1.8 fusion.17
  198.8 1.1 copy-done.8
  199.9 3.5 fusion.3
  203.5 4.7 copy.43
  208.2 3.8 copy.44
  211.9 51.7 %all-to-all-done.3 = bf16[32,8,8,768]{3,2,0,1:T(8,128)(2,1)} async-done(((bf16[32,8,8,768]{3,2,0,1:T(8,128)(2,1)}), bf16[32,8,8,768]{3,2,0,1:T(8,128)(2,1)}, u32[]{:S(2)}, u32[]{:S(2)}) %all-to-all-start.3) | async-done | bytes 3145760 | tf_op jit(solution)/shard_map/all_to_all | solution.py:27
  263.7 5.4 %all-to-all-start.6 = ((bf16[32,8,8,768]{3,2,0,1:T(8,128)(2,1)}), bf16[32,8,8,768]{3,2,0,1:T(8,128)(2,1)}, u32[]{:S(2)}, u32[]{:S(2)}) async-start(bf16[32,8,8,768]{3,2,0,1:T(8,128)(2,1)} %copy.44), calls=%async_computation.6 | async-start | bytes 6291456 | tf_op jit(solution)/shard_map/all_to_all | solution.py:73
  269.1 2.4 copy.38
  271.5 3.2 fusion.6
  274.7 0.9 copy-done.7
  275.6 3.5 fusion.2
  279.1 4.7 copy.40
  283.8 3.7 copy.41
  287.6 51.7 %all-to-all-done.6 = bf16[32,8,8,768]{3,2,0,1:T(8,128)(2,1)} async-done(((bf16[32,8,8,768]{3,2,0,1:T(8,128)(2,1)}), bf16[32,8,8,768]{3,2,0,1:T(8,128)(2,1)}, u32[]{:S(2)}, u32[]{:S(2)}) %all-to-all-start.6) | async-done | bytes 3145760 | tf_op jit(solution)/shard_map/all_to_all | solution.py:73
  339.2 4.5 all-to-all-start.4
  343.7 4.0 copy.45
  347.7 65.3 %all-to-all-done.4 = bf16[32,8,8,768]{3,2,0,1:T(8,128)(2,1)} async-done(((bf16[32,8,8,768]{3,2,0,1:T(8,128)(2,1)}), bf16[32,8,8,768]{3,2,0,1:T(8,128)(2,1)}, u32[]{:S(2)}, u32[]{:S(2)}) %all-to-all-start.4) | async-done | bytes 3145760 | tf_op jit(solution)/shard_map/all_to_all | solution.py:66
  413.0 10.9 %all-to-all-start.7 = ((bf16[32,8,8,768]{3,2,1,0:T(8,128)(2,1)}), bf16[32,8,8,768]{3,2,1,0:T(8,128)(2,1)}, u32[]{:S(2)}, u32[]{:S(2)}) async-start(bf16[32,8,8,768]{3,2,1,0:T(8,128)(2,1)} %copy.45), calls=%async_computation.7 | async-start | bytes 6291456 | tf_op jit(solution)/shard_map/all_to_all | solution.py:72
  423.9 3.9 copy.42
  427.9 35.3 %all-to-all-done.7 = bf16[32,8,8,768]{3,2,1,0:T(8,128)(2,1)} async-done(((bf16[32,8,8,768]{3,2,1,0:T(8,128)(2,1)}), bf16[32,8,8,768]{3,2,1,0:T(8,128)(2,1)}, u32[]{:S(2)}, u32[]{:S(2)}) %all-to-all-start.7) | async-done | bytes 3145760 | tf_op jit(solution)/shard_map/all_to_all | solution.py:72
  463.2 7.3 %all-to-all-start.5 = ((bf16[32,8,8,768]{3,2,1,0:T(8,128)(2,1)}), bf16[32,8,8,768]{3,2,1,0:T(8,128)(2,1)}, u32[]{:S(2)}, u32[]{:S(2)}) async-start(bf16[32,8,8,768]{3,2,1,0:T(8,128)(2,1)} %copy.42), calls=%async_computation.5 | async-start | bytes 6291456 | tf_op jit(solution)/shard_map/all_to_all | solution.py:65
  470.5 2.3 copy.46
  472.8 4.1 fusion.18
  476.9 3.3 add_convert_fusion
  480.2 2.8 copy.49
  483.0 0.6 fusion.1
  483.6 1.5 copy.50
  485.1 24.5 %all-to-all-done.5 = bf16[32,8,8,768]{3,2,1,0:T(8,128)(2,1)} async-done(((bf16[32,8,8,768]{3,2,1,0:T(8,128)(2,1)}), bf16[32,8,8,768]{3,2,1,0:T(8,128)(2,1)}, u32[]{:S(2)}, u32[]{:S(2)}) %all-to-all-start.5) | async-done | bytes 3145760 | tf_op jit(solution)/shard_map/all_to_all | solution.py:65
  509.7 2.8 copy.47
  512.4 0.6 fusion
  513.1 1.5 copy.48
  (19 shorter events, 0.0 us)
Async XLA Ops:
  0.6 196.3 %copy-start = (bf16[512,2048]{1,0:T(8,128)(2,1)S(1)}, bf16[512,2048]{1,0:T(8,128)(2,1)}, u32[]{:S(2)}) copy-start(bf16[512,2048]{1,0:T(8,128)(2,1)} %param.7) | copy-start | bytes 6291460
  62.5 44.1 %all-to-all-start.2 = ((bf16[32,8,8,768]{3,2,1,0:T(8,128)(2,1)}), bf16[32,8,8,768]{3,2,1,0:T(8,128)(2,1)}, u32[]{:S(2)}, u32[]{:S(2)}) async-start(bf16[32,8,8,768]{3,2,1,0:T(8,128)(2,1)} %bitcast.65), calls=%async_computation.2 | async-start | bytes 6291456 | tf_op jit(solution)/shard_map/all_to_all | solution.py:28
  106.6 82.4 %all-to-all-start.1 = ((bf16[32,8,8,768]{3,2,0,1:T(8,128)(2,1)}), bf16[32,8,8,768]{3,2,0,1:T(8,128)(2,1)}, u32[]{:S(2)}, u32[]{:S(2)}) async-start(bf16[32,8,8,768]{3,2,0,1:T(8,128)(2,1)} %copy.35), calls=%async_computation.1 | async-start | bytes 6291456 | tf_op jit(solution)/shard_map/all_to_all | solution.py:20
  118.6 74.9 %copy-start.4 = (bf16[512,768]{1,0:T(8,128)(2,1)S(1)}, bf16[512,768]{1,0:T(8,128)(2,1)}, u32[]{:S(2)}) copy-start(bf16[512,768]{1,0:T(8,128)(2,1)} %param.8) | copy-start | bytes 2359300
  189.0 74.7 %all-to-all-start.3 = ((bf16[32,8,8,768]{3,2,0,1:T(8,128)(2,1)}), bf16[32,8,8,768]{3,2,0,1:T(8,128)(2,1)}, u32[]{:S(2)}, u32[]{:S(2)}) async-start(bf16[32,8,8,768]{3,2,0,1:T(8,128)(2,1)} %copy.37), calls=%async_computation.3 | async-start | bytes 6291456 | tf_op jit(solution)/shard_map/all_to_all | solution.py:27
  196.9 1.9 copy-start.1
  196.9 3.0 copy-start.5
  198.8 1.1 copy-start.8
  263.7 75.6 %all-to-all-start.6 = ((bf16[32,8,8,768]{3,2,0,1:T(8,128)(2,1)}), bf16[32,8,8,768]{3,2,0,1:T(8,128)(2,1)}, u32[]{:S(2)}, u32[]{:S(2)}) async-start(bf16[32,8,8,768]{3,2,0,1:T(8,128)(2,1)} %copy.44), calls=%async_computation.6 | async-start | bytes 6291456 | tf_op jit(solution)/shard_map/all_to_all | solution.py:73
  269.1 2.4 copy-start.9
  271.5 3.2 copy-start.2
  274.7 0.9 copy-start.7
  339.2 73.8 %all-to-all-start.4 = ((bf16[32,8,8,768]{3,2,0,1:T(8,128)(2,1)}), bf16[32,8,8,768]{3,2,0,1:T(8,128)(2,1)}, u32[]{:S(2)}, u32[]{:S(2)}) async-start(bf16[32,8,8,768]{3,2,0,1:T(8,128)(2,1)} %copy.41), calls=%async_computation.4 | async-start | bytes 6291456 | tf_op jit(solution)/shard_map/all_to_all | solution.py:66
  413.0 50.2 %all-to-all-start.7 = ((bf16[32,8,8,768]{3,2,1,0:T(8,128)(2,1)}), bf16[32,8,8,768]{3,2,1,0:T(8,128)(2,1)}, u32[]{:S(2)}, u32[]{:S(2)}) async-start(bf16[32,8,8,768]{3,2,1,0:T(8,128)(2,1)} %copy.45), calls=%async_computation.7 | async-start | bytes 6291456 | tf_op jit(solution)/shard_map/all_to_all | solution.py:72
  463.2 46.5 %all-to-all-start.5 = ((bf16[32,8,8,768]{3,2,1,0:T(8,128)(2,1)}), bf16[32,8,8,768]{3,2,1,0:T(8,128)(2,1)}, u32[]{:S(2)}, u32[]{:S(2)}) async-start(bf16[32,8,8,768]{3,2,1,0:T(8,128)(2,1)} %copy.42), calls=%async_computation.5 | async-start | bytes 6291456 | tf_op jit(solution)/shard_map/all_to_all | solution.py:65
  472.7 4.1 copy-start.3
  472.7 4.1 copy-start.10
  480.2 2.8 copy-start.6
where the time goes:
time: 516 us; the launch traced here: 515 us
  waiting for transfers between devices  334 us (65%)
  local copies, waits for them, and re-layouts  58.9 us (11%)
  blocking collectives  48.1 us (9%)
  starting transfers between devices  45.6 us (9%)
  matrix products  20.7 us (4%)
  other arithmetic  6.06 us (1%)
    all_to_all x1, waiting for transfers between devices, per_device(): lax.all_to_all(lax.all_to_all(outgoing[0], 'expert', split_axis=0, concat...  70.4 us
    all_to_all x1, waiting for transfers between devices, per_device(): lax.all_to_all(part_gate, 'replica', split_axis=1, concat_axis=1, tiled=T...  65.3 us
    all_to_all x1, waiting for transfers between devices, per_device(): lax.all_to_all(lax.all_to_all(outgoing[1], 'expert', split_axis=0, concat...  51.7 us
    all_to_all x1, waiting for transfers between devices, per_device(): lax.all_to_all(part_up, 'replica', split_axis=1, concat_axis=1, tiled=True)  51.7 us
    all_to_all x1, blocking collectives, per_device(): lax.all_to_all(outgoing[0], 'expert', split_axis=0, concat_axis=0, tiled=...  48.1 us
    all_to_all x1, waiting for transfers between devices, per_device(): lax.all_to_all(outgoing[1], 'expert', split_axis=0, concat_axis=0, tiled=...  35.5 us
    all_to_all x1, waiting for transfers between devices, per_device(): lax.all_to_all(lax.all_to_all(part_up, 'replica', split_axis=1, concat_ax...  35.3 us
    all_to_all x1, waiting for transfers between devices, per_device(): lax.all_to_all(lax.all_to_all(part_gate, 'replica', split_axis=1, concat_...  24.5 us
  transfers between devices with their start and end apart: 7, of which 7 were waited for; matrix products, arithmetic and copies ran while one was open for 13% of the time, Pallas kernels for 0%

commit v1 on v0

v1 whole, which is shorter than its diff:
```python
import jax
import jax.numpy as jnp
from jax import lax
from jax.sharding import PartitionSpec as P

BOTH = ("expert", "replica")


def exchange(parts):
    return lax.all_to_all(parts, BOTH, split_axis=0, concat_axis=0, tiled=True)


def per_device(tokens, d_hidden, w_gate, w_up, expert_ids):
    expert_total, block_rows, width = w_gate.shape
    block_count = expert_ids.shape[0]
    model_width = block_count * block_rows
    both = jnp.concatenate([w_gate, w_up], axis=2)
    outgoing = both.at[expert_ids].get(mode="promise_in_bounds")
    weights = exchange(outgoing).reshape(model_width, 2 * width)
    pre = jnp.dot(tokens, weights, preferred_element_type=jnp.float32)
    gate_pre, up_pre = pre[:, :width], pre[:, width:]
    sig = jax.nn.sigmoid(gate_pre)
    activated = gate_pre * sig
    hidden = (activated * up_pre).astype(jnp.bfloat16)
    upstream = d_hidden.astype(jnp.float32)
    d_gate = upstream * up_pre * sig * (1.0 + gate_pre * (1.0 - sig))
    d_up = upstream * activated
    d_both = jnp.concatenate([d_gate, d_up], axis=1).astype(jnp.bfloat16)
    part = lax.dot_general(
        tokens, d_both, (((0,), (0,)), ((), ())), preferred_element_type=jnp.float32
    ).astype(jnp.bfloat16)
    terms = exchange(part.reshape(block_count, block_rows, 2 * width))
    token_grad = lax.dot_general(
        d_both, weights, (((1,), (1,)), ((), ())), preferred_element_type=jnp.float32
    ).astype(jnp.bfloat16)
    selector = (expert_ids[None, :] == jnp.arange(expert_total, dtype=jnp.int32)[:, None]).astype(jnp.bfloat16)
    scale = tokens.shape[0] ** (-0.5)
    grad = jnp.dot(selector, terms.reshape(block_count, -1), preferred_element_type=jnp.float32) * scale
    grad = grad.astype(jnp.bfloat16).reshape(expert_total, block_rows, 2 * width)
    return hidden, token_grad, grad[:, :, :width], grad[:, :, width:]


def solution(mesh):
    rows, weights = P(BOTH, None), P(None, BOTH, None)
    return jax.shard_map(
        per_device,
        mesh=mesh,
        in_specs=(rows, rows, weights, weights, P()),
        out_specs=(rows, rows, weights, weights),
        check_vma=False,
    )
```

time: 516 us -> 360 us (0.70)
  waiting for transfers between devices: 334 us -> 274 us
  blocking collectives: 48.1 us -> 0 us
  local copies, waits for them, and re-layouts: 58.9 us -> 29.7 us
  starting transfers between devices: 45.6 us -> 23.8 us
    all_to_all x7 -> x2, waiting for transfers between devices: 334 us -> 274 us  [exchange(): return lax.all_to_all(parts, BOTH, split_axis=0, concat_axis=0, tiled=True)]
    all_to_all x1 -> x0, blocking collectives: 48.1 us -> none  [per_device(): lax.all_to_all(outgoing[0], 'expert', split_axis=0, concat_axis=0, tiled=...]
    all_to_all x7 -> x2, starting transfers between devices: 45.6 us -> 23.8 us  [exchange(): return lax.all_to_all(parts, BOTH, split_axis=0, concat_axis=0, tiled=True)]
    all_to_all x6 -> x1, local copies, waits for them, and re-layouts: 20.2 us -> 9.11 us  [exchange(): return lax.all_to_all(parts, BOTH, split_axis=0, concat_axis=0, tiled=True)]
    unnamed x28 -> x15, local copies, waits for them, and re-layouts: 14.1 us -> 4.62 us
    reshape x2 -> x0, local copies, waits for them, and re-layouts: 7.5 us -> none  [the longest x1 3.76 us: per_device(): part_up = lax.dot_general(tokens, d_up, outer_dims, preferred_element_typ...]
    dot_general x8 -> x4, matrix products: 20.7 us -> 25 us  [the longest x1 8.07 us: per_device(): lax.dot_general(d_both, weights, (((1,), (1,)), ((), ())), preferred_elem...]
  transfers between devices with their start and end apart: 7 -> 2, of which waited for: 7 -> 2; matrix products, arithmetic and copies ran while one was open for 13% -> 3% of each run, Pallas kernels for 0% -> 0%
where the time goes in v1:
time: 360 us; the launch traced here: 359 us
  waiting for transfers between devices  274 us (76%)
  local copies, waits for them, and re-layouts  29.7 us (8%)
  matrix products  25 us (7%)
  starting transfers between devices  23.8 us (7%)
  other arithmetic  5.65 us (2%)
    all_to_all x2, waiting for transfers between devices, exchange(): return lax.all_to_all(parts, BOTH, split_axis=0, concat_axis=0, tiled=True)  274 us
    all_to_all x2, starting transfers between devices, exchange(): return lax.all_to_all(parts, BOTH, split_axis=0, concat_axis=0, tiled=True)  23.8 us
    all_to_all x1, local copies, waits for them, and re-layouts, exchange(): return lax.all_to_all(parts, BOTH, split_axis=0, concat_axis=0, tiled=True)  9.11 us
    convert_element_type x1, local copies, waits for them, and re-layouts, per_device(): part = lax.dot_general(tokens, d_both, (((0,), (0,)), ((), ())), preferre...  8.62 us
    dot_general x1, matrix products, per_device(): lax.dot_general(d_both, weights, (((1,), (1,)), ((), ())), preferred_elem...  8.07 us
  transfers between devices with their start and end apart: 2, of which 2 were waited for; matrix products, arithmetic and copies ran while one was open for 3% of the time, Pallas kernels for 0%

profile of v1, /device:TPU:1, one launch (start us, length us, event | category | flops | bytes accessed | tf_op | source)
XLA Modules:
  0.0 359.1 jit_solution(1024011955380179339)
XLA Ops:
  0.6 0.0 copy-start
  0.6 0.8 compare_select_fusion
  1.5 3.7 %pad_maximum_fusion = bf16[128,8,1536]{2,1,0:T(8,128)(2,1)} fusion(bf16[128,8,768]{2,1,0:T(8,128)(2,1)} %param.8, bf16[128,8,768]{2,1,0:T(8,128)(2,1)} %param.7), kind=kLoop, calls=%fused_computation.10 | loop fusion | flops 6291456 | bytes 6291456 | tf_op jit(solution)/shard_map/concatenate | solution.py:17
  5.2 5.5 %gather_fusion = bf16[256,8,1536]{2,1,0:T(8,128)(2,1)} fusion(bf16[128,8,1536]{2,1,0:T(8,128)(2,1)} %pad_maximum_fusion, s32[1024]{0:T(1024)S(1)} %pad_clamp_fusion), kind=kCustom, calls=%fused_computation | custom fusion | bytes 12583936 | tf_op jit(solution)/shard_map/gather | solution.py:18
  10.7 0.0 copy-start.4
  10.7 16.5 %all-to-all-start = ((bf16[256,8,1536]{2,1,0:T(8,128)(2,1)}), bf16[256,8,1536]{2,1,0:T(8,128)(2,1)}, u32[]{:S(2)}, u32[]{:S(2)}) async-start(bf16[256,8,1536]{2,1,0:T(8,128)(2,1)} %gather_fusion), calls=%async_computation | async-start | bytes 12582912 | tf_op jit(solution)/shard_map/all_to_all | solution.py:10
  27.3 0.0 copy-done.4
  27.3 1.2 copy.11
  28.4 141.1 %all-to-all-done = bf16[256,8,1536]{2,1,0:T(8,128)(2,1)} async-done(((bf16[256,8,1536]{2,1,0:T(8,128)(2,1)}), bf16[256,8,1536]{2,1,0:T(8,128)(2,1)}, u32[]{:S(2)}, u32[]{:S(2)}) %all-to-all-start) | async-done | bytes 6291488 | tf_op jit(solution)/shard_map/all_to_all | solution.py:10
  169.5 0.0 copy-done
  169.5 0.0 copy-start.1
  169.5 5.7 %fusion.6 = f32[512,1536]{0,1:T(8,128)S(1)} fusion(bf16[512,2048]{1,0:T(8,128)(2,1)S(1)} %copy-done, bf16[256,8,1536]{2,1,0:T(8,128)(2,1)} %all-to-all-done), kind=kOutput, calls=%fused_computation.9 | convolution fusion | flops 3221225472 | bytes 11534336 | tf_op jit(solution)/shard_map/dot_general | solution.py:20
  175.2 0.0 copy-done.1
  175.2 1.1 fusion.14
  176.3 0.0 copy-start.2
  176.3 0.0 copy-start.3
  176.3 0.9 copy-done.2
  177.2 0.3 copy-done.3
  177.4 6.3 %fusion.1 = bf16[2048,1536]{0,1:T(8,128)(2,1)} fusion(bf16[512,2048]{1,0:T(8,128)(2,1)S(1)} %copy-done, bf16[512,768]{0,1:T(8,128)(2,1)S(1)} %get-tuple-element.13, bf16[512,768]{0,1:T(8,128)(2,1)S(1)} %get-tuple-element.12), kind=kOutput, calls=%fused_computation.4 | convolution fusion | flops 3227516928 | bytes 9961472 | tf_op jit(solution)/shard_map/dot_general | solution.py:29
  183.8 8.6 %copy.12 = bf16[2048,1536]{1,0:T(8,128)(2,1)} copy(bf16[2048,1536]{0,1:T(8,128)(2,1)} %fusion.1) | data formatting | bytes 12582912 | tf_op jit(solution)/shard_map/convert_element_type | solution.py:31
  192.4 7.3 %all-to-all-start.1 = ((bf16[256,8,1536]{2,1,0:T(8,128)(2,1)}), bf16[256,8,1536]{2,1,0:T(8,128)(2,1)}, u32[]{:S(2)}, u32[]{:S(2)}) async-start(bf16[256,8,1536]{2,1,0:T(8,128)(2,1)} %bitcast.20), calls=%async_computation.1 | async-start | bytes 12582912 | tf_op jit(solution)/shard_map/all_to_all | solution.py:10
  199.7 1.2 copy.14
  200.9 8.1 %fusion.9 = bf16[512,2048]{1,0:T(8,128)(2,1)} fusion(bf16[256,8,1536]{2,1,0:T(8,128)(2,1)} %all-to-all-done, bf16[512,768]{0,1:T(8,128)(2,1)} %copy-done.3, bf16[512,768]{0,1:T(8,128)(2,1)} %copy-done.2), kind=kOutput, calls=%fused_computation.11 | convolution fusion | flops 3225419776 | bytes 9961472 | tf_op jit(solution)/shard_map/dot_general | solution.py:33
  208.9 0.0 copy-start.5
  208.9 133.0 %all-to-all-done.1 = bf16[256,8,1536]{2,1,0:T(8,128)(2,1)} async-done(((bf16[256,8,1536]{2,1,0:T(8,128)(2,1)}), bf16[256,8,1536]{2,1,0:T(8,128)(2,1)}, u32[]{:S(2)}, u32[]{:S(2)}) %all-to-all-start.1) | async-done | bytes 6291488 | tf_op jit(solution)/shard_map/all_to_all | solution.py:10
  342.0 9.1 %copy.13 = bf16[256,8,1536]{0,2,1:T(8,128)(2,1)} copy(bf16[256,8,1536]{2,1,0:T(8,128)(2,1)} %all-to-all-done.1) | data formatting | bytes 12582912 | tf_op jit(solution)/shard_map/all_to_all | solution.py:10
  351.1 0.0 copy-done.5
  351.1 4.9 %fusion = bf16[128,12288]{1,0:T(8,128)(2,1)S(1)} fusion(bf16[256,12288]{0,1:T(8,128)(2,1)} %bitcast.21, s32[256]{0:T(256)S(1)} %copy-done.5), kind=kOutput, calls=%fused_computation.2 | convolution fusion | flops 808484864 | bytes 9438208 | tf_op jit(solution)/shard_map/dot_general | solution.py:38
  356.0 1.2 copy.15
  357.2 1.9 fusion.20
  (1 shorter events, 0.0 us)
Async XLA Ops:
  0.6 168.9 %copy-start = (bf16[512,2048]{1,0:T(8,128)(2,1)S(1)}, bf16[512,2048]{1,0:T(8,128)(2,1)}, u32[]{:S(2)}) copy-start(bf16[512,2048]{1,0:T(8,128)(2,1)} %param.5) | copy-start | bytes 6291460
  10.7 16.5 %copy-start.4 = (bf16[512,768]{1,0:T(8,128)(2,1)S(1)}, bf16[512,768]{1,0:T(8,128)(2,1)}, u32[]{:S(2)}) copy-start(bf16[512,768]{1,0:T(8,128)(2,1)} %param.6) | copy-start | bytes 2359300
  10.7 158.8 %all-to-all-start = ((bf16[256,8,1536]{2,1,0:T(8,128)(2,1)}), bf16[256,8,1536]{2,1,0:T(8,128)(2,1)}, u32[]{:S(2)}, u32[]{:S(2)}) async-start(bf16[256,8,1536]{2,1,0:T(8,128)(2,1)} %gather_fusion), calls=%async_computation | async-start | bytes 12582912 | tf_op jit(solution)/shard_map/all_to_all | solution.py:10
  169.5 5.7 %copy-start.1 = (bf16[512,768]{0,1:T(8,128)(2,1)S(1)}, bf16[512,768]{0,1:T(8,128)(2,1)}, u32[]{:S(2)}) copy-start(bf16[512,768]{0,1:T(8,128)(2,1)} %copy.11) | copy-start | bytes 2359300
  176.3 0.9 copy-start.2
  176.3 1.1 copy-start.3
  192.4 149.6 %all-to-all-start.1 = ((bf16[256,8,1536]{2,1,0:T(8,128)(2,1)}), bf16[256,8,1536]{2,1,0:T(8,128)(2,1)}, u32[]{:S(2)}, u32[]{:S(2)}) async-start(bf16[256,8,1536]{2,1,0:T(8,128)(2,1)} %bitcast.20), calls=%async_computation.1 | async-start | bytes 12582912 | tf_op jit(solution)/shard_map/all_to_all | solution.py:10
  208.9 142.2 %copy-start.5 = (s32[256]{0:T(256)S(1)}, s32[256]{0:T(256)}, u32[]{:S(2)}) copy-start(s32[256]{0:T(256)} %param.9) | copy-start | bytes 3076

commit v2 on v1

v2 whole, which is shorter than its diff:
```python
import jax
import jax.numpy as jnp
from jax import lax
from jax.experimental import pallas as pl
from jax.experimental.pallas import tpu as pltpu
from jax.sharding import PartitionSpec as P

BOTH = ("expert", "replica")
F32, BF16 = jnp.float32, jnp.bfloat16
MIB = 1 << 20


def each(n, body, unroll=1):
    def step(s, carry):
        body(s)
        return carry

    lax.fori_loop(0, n, step, 0, unroll=unroll)


def gather_rows(ids, w_gate, w_up):
    experts, r, width = w_gate.shape
    blocks = ids.shape[0]
    steps = 4
    share = blocks // steps

    def body(ids, gate, up, out):
        first = pl.program_id(0) * share

        def one(b):
            j = ids[first + b]
            out[b, :, :width] = gate[j]
            out[b, :, width:] = up[j]

        each(share, one, 4)

    whole = pl.BlockSpec((experts, r, width), lambda i, ids: (0, 0, 0))
    return pl.pallas_call(
        body,
        out_shape=jax.ShapeDtypeStruct((blocks, r, 2 * width), BF16),
        grid_spec=pltpu.PrefetchScalarGridSpec(
            num_scalar_prefetch=1,
            grid=(steps,),
            in_specs=[whole, whole],
            out_specs=pl.BlockSpec((share, r, 2 * width), lambda i, ids: (i, 0, 0)),
        ),
        compiler_params=pltpu.CompilerParams(vmem_limit_bytes=24 * MIB),
        name="gather_rows",
    )(ids, w_gate, w_up)


def block_compute(tokens, tokens_t, d_hidden, weights):
    rows, model = tokens.shape
    width = d_hidden.shape[1]
    n_rows, n_model = 4, 4
    tr, tm = rows // n_rows, model // n_model

    def body(x, xt, dh, w, h_out, d_out, part_out, dd):
        i = pl.program_id(0)

        @pl.when(i < n_rows)
        def _():
            pre = jnp.dot(x[...], w[...], preferred_element_type=F32)
            gate, up = pre[:, :width], pre[:, width:]
            sig = jax.nn.sigmoid(gate)
            act = gate * sig
            h_out[...] = (act * up).astype(BF16)
            g = dh[...].astype(F32)
            at = pl.ds(pl.multiple_of(i * tr, tr), tr)
            dg = (g * up * sig * (1.0 + gate * (1.0 - sig))).astype(BF16)
            du = (g * act).astype(BF16)
            dd[at, :width] = dg
            dd[at, width:] = du
            d_out[:, :width] = dg
            d_out[:, width:] = du

        @pl.when(i >= n_rows)
        def _():
            part_out[...] = jnp.dot(xt[...], dd[...], preferred_element_type=F32).astype(BF16)

    def early(i):
        return jnp.minimum(i, n_rows - 1)

    def late(i):
        return jnp.maximum(i - n_rows, 0)

    return pl.pallas_call(
        body,
        out_shape=[
            jax.ShapeDtypeStruct((rows, width), BF16),
            jax.ShapeDtypeStruct((rows, 2 * width), BF16),
            jax.ShapeDtypeStruct((model, 2 * width), BF16),
        ],
        grid=(n_rows + n_model,),
        in_specs=[
            pl.BlockSpec((tr, model), lambda i: (early(i), 0)),
            pl.BlockSpec((tm, rows), lambda i: (late(i), 0)),
            pl.BlockSpec((tr, width), lambda i: (early(i), 0)),
            pl.BlockSpec((model, 2 * width), lambda i: (0, 0)),
        ],
        out_specs=[
            pl.BlockSpec((tr, width), lambda i: (early(i), 0)),
            pl.BlockSpec((tr, 2 * width), lambda i: (early(i), 0)),
            pl.BlockSpec((tm, 2 * width), lambda i: (late(i), 0)),
        ],
        scratch_shapes=[pltpu.VMEM((rows, 2 * width), BF16)],
        compiler_params=pltpu.CompilerParams(vmem_limit_bytes=40 * MIB),
        cost_estimate=pl.CostEstimate(
            flops=8 * rows * model * width, bytes_accessed=20 * MIB, transcendentals=rows * width
        ),
        name="block_compute",
    )(tokens, tokens_t, d_hidden, weights)


def token_gradient(d_both, weights):
    rows, deep = d_both.shape
    model = weights.shape[0]
    tile = min(256, model)

    def body(d, w, out):
        out[...] = lax.dot_general(
            d[...], w[...], (((1,), (1,)), ((), ())), preferred_element_type=F32
        ).astype(BF16)

    return pl.pallas_call(
        body,
        out_shape=jax.ShapeDtypeStruct((rows, model), BF16),
        grid=(model // tile,),
        in_specs=[pl.BlockSpec((rows, deep), lambda i: (0, 0)), pl.BlockSpec((tile, deep), lambda i: (i, 0))],
        out_specs=pl.BlockSpec((rows, tile), lambda i: (0, i)),
        compiler_params=pltpu.CompilerParams(vmem_limit_bytes=24 * MIB),
        cost_estimate=pl.CostEstimate(flops=2 * rows * model * deep, bytes_accessed=10 * MIB, transcendentals=0),
        name="token_gradient",
    )(d_both, weights)


def sum_terms(ids, terms, experts, width, scale):
    blocks, r, _ = terms.shape
    steps = 3
    w = width // steps

    def body(ids, gate, up, gate_out, up_out, gate_sum, up_sum):
        gate_sum[...] = jnp.zeros_like(gate_sum)
        up_sum[...] = jnp.zeros_like(up_sum)

        def one(b):
            j = ids[b]
            gate_sum[j] = gate_sum[j] + gate[b].astype(F32)
            up_sum[j] = up_sum[j] + up[b].astype(F32)

        each(blocks, one, 4)
        gate_out[...] = (gate_sum[...] * scale).astype(BF16)
        up_out[...] = (up_sum[...] * scale).astype(BF16)

    def cols(n, first):
        return pl.BlockSpec((n, r, w), lambda i, ids: (0, 0, first + i))

    return pl.pallas_call(
        body,
        out_shape=[jax.ShapeDtypeStruct((experts, r, width), BF16)] * 2,
        grid_spec=pltpu.PrefetchScalarGridSpec(
            num_scalar_prefetch=1,
            grid=(steps,),
            in_specs=[cols(blocks, 0), cols(blocks, steps)],
            out_specs=[cols(experts, 0)] * 2,
            scratch_shapes=[pltpu.VMEM((experts, r, w), F32)] * 2,
        ),
        compiler_params=pltpu.CompilerParams(vmem_limit_bytes=24 * MIB),
        name="sum_terms",
    )(ids, terms, terms)


def exchange(parts):
    return lax.all_to_all(parts, BOTH, split_axis=0, concat_axis=0, tiled=True)


def per_device(tokens, d_hidden, w_gate, w_up, expert_ids):
    experts, r, width = w_gate.shape
    blocks = expert_ids.shape[0]
    model = blocks * r
    weights = exchange(gather_rows(expert_ids, w_gate, w_up)).reshape(model, 2 * width)
    tokens_t = lax.optimization_barrier(tokens.T)
    hidden, d_both, part = block_compute(tokens, tokens_t, d_hidden, weights)
    terms = exchange(part.reshape(blocks, r, 2 * width))
    token_grad = token_gradient(d_both, weights)
    grad_gate, grad_up = sum_terms(expert_ids, terms, experts, width, tokens.shape[0] ** (-0.5))
    return hidden, token_grad, grad_gate, grad_up


def solution(mesh):
    rows, weights = P(BOTH, None), P(None, BOTH, None)
    return jax.shard_map(
        per_device,
        mesh=mesh,
        in_specs=(rows, rows, weights, weights, P()),
        out_specs=(rows, rows, weights, weights),
        check_vma=False,
    )
```

time: 360 us -> 342 us (0.950)
  Pallas kernels: 0 us -> 30 us
  matrix products: 25 us -> 0 us
  local copies, waits for them, and re-layouts: 29.7 us -> 14 us
  other arithmetic: 5.65 us -> 0 us
    pallas_call x0 -> x4, Pallas kernels: none -> 30 us  [the longest x1 11.8 us: block_compute(): pl.pallas_call(body, out_shape=[jax.ShapeDtypeStruct((rows, width), BF16)...]
    dot_general x4 -> x0, matrix products: 25 us -> none  [the longest x1 8.07 us: per_device(): lax.dot_general(d_both, weights, (((1,), (1,)), ((), ())), preferred_elem...]
    unnamed x15 -> x23, local copies, waits for them, and re-layouts: 4.62 us -> 14 us
    all_to_all x1 -> x0, local copies, waits for them, and re-layouts: 9.11 us -> none  [exchange(): return lax.all_to_all(parts, BOTH, split_axis=0, concat_axis=0, tiled=True)]
    convert_element_type x1 -> x0, local copies, waits for them, and re-layouts: 8.62 us -> none  [per_device(): part = lax.dot_general(tokens, d_both, (((0,), (0,)), ((), ())), preferre...]
    gather x1 -> x0, local copies, waits for them, and re-layouts: 5.5 us -> none  [per_device(): outgoing = both.at[expert_ids].get(mode='promise_in_bounds')]
    concatenate x1 -> x0, other arithmetic: 3.73 us -> none  [per_device(): both = jnp.concatenate([w_gate, w_up], axis=2)]
  transfers between devices with their start and end apart: 2 -> 2, of which waited for: 2 -> 2; matrix products, arithmetic and copies ran while one was open for 3% -> 1% of each run, Pallas kernels for 0% -> 3%
where the time goes in v2:
time: 342 us
  waiting for transfers between devices  273 us (80%)
  Pallas kernels  30 us (9%)
  starting transfers between devices  23.8 us (7%)
  local copies, waits for them, and re-layouts  14 us (4%)
    all_to_all x2, waiting for transfers between devices, exchange(): return lax.all_to_all(parts, BOTH, split_axis=0, concat_axis=0, tiled=True)  273 us
    all_to_all x2, starting transfers between devices, exchange(): return lax.all_to_all(parts, BOTH, split_axis=0, concat_axis=0, tiled=True)  23.8 us
    unnamed x23, local copies, waits for them, and re-layouts  14 us
    pallas_call x1, Pallas kernels, block_compute(): pl.pallas_call(body, out_shape=[jax.ShapeDtypeStruct((rows, width), BF16)...  11.8 us
    pallas_call x1, Pallas kernels, token_gradient(): pl.pallas_call(body, out_shape=jax.ShapeDtypeStruct((rows, model), BF16),...  8.79 us
    pallas_call x1, Pallas kernels, sum_terms(): pl.pallas_call(body, out_shape=[jax.ShapeDtypeStruct((experts, r, width),...  7.98 us
  transfers between devices with their start and end apart: 2, of which 2 were waited for; matrix products, arithmetic and copies ran while one was open for 1% of the time, Pallas kernels for 3%

profile of v2, /device:TPU:1, one launch (start us, length us, event | category | flops | bytes accessed | tf_op | source)
XLA Modules:
  0.0 341.7 jit_solution(169498791350563413)
XLA Ops:
  0.6 0.0 copy-start.4
  0.6 1.4 copy-done.4
  2.0 0.0 copy-start.5
  2.0 1.4 copy-done.5
  3.4 0.0 copy-start.6
  3.5 0.7 copy-done.6
  4.1 1.4 gather_rows.1
  5.6 0.0 copy-start
  5.6 2.6 copy-done
  8.2 0.0 copy-start.2
  8.2 16.5 %all-to-all-start = ((bf16[256,8,1536]{2,1,0:T(8,128)(2,1)}), bf16[256,8,1536]{2,1,0:T(8,128)(2,1)}, u32[]{:S(2)}, u32[]{:S(2)}) async-start(bf16[256,8,1536]{2,1,0:T(8,128)(2,1)} %copy-done), calls=%async_computation | async-start | bytes 12582912 | tf_op jit(solution)/shard_map/all_to_all | solution.py:174
  24.7 0.0 copy-done.2
  24.7 0.0 copy-start.8
  24.8 2.5 copy.9
  27.3 139.7 %all-to-all-done = bf16[256,8,1536]{2,1,0:T(8,128)(2,1)} async-done(((bf16[256,8,1536]{2,1,0:T(8,128)(2,1)}), bf16[256,8,1536]{2,1,0:T(8,128)(2,1)}, u32[]{:S(2)}, u32[]{:S(2)}) %all-to-all-start) | async-done | bytes 6291488 | tf_op jit(solution)/shard_map/all_to_all | solution.py:174
  167.0 0.0 copy-done.8
  167.0 0.0 copy-start.3
  167.0 1.6 copy-done.3
  168.6 11.8 %block_compute.1 = (bf16[512,768]{1,0:T(8,128)(2,1)}, bf16[512,1536]{1,0:T(8,128)(2,1)S(1)}, bf16[2048,1536]{1,0:T(8,128)(2,1)S(1)}) custom-call(bf16[512,2048]{1,0:T(8,128)(2,1)S(1)} %copy-done.2, bf16[2048,512]{1,0:T(8,128)(2,1)S(1)} %bitcast.4, bf16[512,768]{1,0:T(8,128)(2,1)S(1)} %copy-done.8, bf16[2048,1536]{1,0:T(8,128)(2,1)} %bitcast.1.w), custom_call_target="tpu_custom_call" | custom-call | flops 6442450944 | bytes 20971520 | tf_op jit(solution)/shard_map/block_compute/pallas_call | solution.py:87
  180.4 0.0 copy-start.1
  180.4 2.6 copy-done.1
  183.0 0.0 copy-start.9
  183.0 1.1 copy-done.9
  184.2 0.0 copy-start.10
  184.2 7.3 %all-to-all-start.1 = ((bf16[256,8,1536]{2,1,0:T(8,128)(2,1)}), bf16[256,8,1536]{2,1,0:T(8,128)(2,1)}, u32[]{:S(2)}, u32[]{:S(2)}) async-start(bf16[256,8,1536]{2,1,0:T(8,128)(2,1)} %bitcast.3), calls=%async_computation.1 | async-start | bytes 12582912 | tf_op jit(solution)/shard_map/all_to_all | solution.py:174
  191.5 0.0 copy-done.10
  191.5 0.0 copy-start.7
  191.5 8.8 %token_gradient.1 = bf16[512,2048]{1,0:T(8,128)(2,1)} custom-call(bf16[512,1536]{1,0:T(8,128)(2,1)S(1)} %copy-done.10, bf16[2048,1536]{1,0:T(8,128)(2,1)} %bitcast.1.w), custom_call_target="tpu_custom_call" | custom-call | flops 3221225472 | bytes 10485760 | tf_op jit(solution)/shard_map/token_gradient/pallas_call | solution.py:125
  200.3 133.5 %all-to-all-done.1.gate.up = bf16[256,8,1536]{2,1,0:T(8,128)(2,1)} async-done(((bf16[256,8,1536]{2,1,0:T(8,128)(2,1)}), bf16[256,8,1536]{2,1,0:T(8,128)(2,1)}, u32[]{:S(2)}, u32[]{:S(2)}) %all-to-all-start.1) | async-done | bytes 6291488 | tf_op jit(solution)/shard_map/all_to_all | solution.py:174
  333.7 0.0 copy-done.7
  333.8 8.0 %sum_terms.1 = (bf16[128,8,768]{2,1,0:T(8,128)(2,1)}, bf16[128,8,768]{2,1,0:T(8,128)(2,1)}) custom-call(s32[256]{0:T(256)S(1)} %copy-done.7, bf16[256,8,1536]{2,1,0:T(8,128)(2,1)} %all-to-all-done.1.gate.up, bf16[256,8,1536]{2,1,0:T(8,128)(2,1)} %all-to-all-done.1.gate.up), custom_call_target="tpu_custom_call" | custom-call | tf_op jit(solution)/shard_map/sum_terms/pallas_call | solution.py:158
Async XLA Ops:
  0.6 1.4 copy-start.4
  2.0 1.4 copy-start.5
  3.4 0.7 copy-start.6
  5.6 2.6 copy-start
  8.2 16.5 %copy-start.2 = (bf16[512,2048]{1,0:T(8,128)(2,1)S(1)}, bf16[512,2048]{1,0:T(8,128)(2,1)}, u32[]{:S(2)}) copy-start(bf16[512,2048]{1,0:T(8,128)(2,1)} %x.1) | copy-start | bytes 6291460
  8.2 158.8 %all-to-all-start = ((bf16[256,8,1536]{2,1,0:T(8,128)(2,1)}), bf16[256,8,1536]{2,1,0:T(8,128)(2,1)}, u32[]{:S(2)}, u32[]{:S(2)}) async-start(bf16[256,8,1536]{2,1,0:T(8,128)(2,1)} %copy-done), calls=%async_computation | async-start | bytes 12582912 | tf_op jit(solution)/shard_map/all_to_all | solution.py:174
  24.7 142.3 %copy-start.8 = (bf16[512,768]{1,0:T(8,128)(2,1)S(1)}, bf16[512,768]{1,0:T(8,128)(2,1)}, u32[]{:S(2)}) copy-start(bf16[512,768]{1,0:T(8,128)(2,1)} %dh.1) | copy-start | bytes 2359300
  167.0 1.6 copy-start.3
  180.4 2.6 copy-start.1
  183.0 1.1 copy-start.9
  184.2 7.3 %copy-start.10 = (bf16[512,1536]{1,0:T(8,128)(2,1)S(1)}, bf16[512,1536]{1,0:T(8,128)(2,1)}, u32[]{:S(2)}) copy-start(bf16[512,1536]{1,0:T(8,128)(2,1)} %copy-done.9) | copy-start | bytes 4718596
  184.2 149.6 %all-to-all-start.1 = ((bf16[256,8,1536]{2,1,0:T(8,128)(2,1)}), bf16[256,8,1536]{2,1,0:T(8,128)(2,1)}, u32[]{:S(2)}, u32[]{:S(2)}) async-start(bf16[256,8,1536]{2,1,0:T(8,128)(2,1)} %bitcast.3), calls=%async_computation.1 | async-start | bytes 12582912 | tf_op jit(solution)/shard_map/all_to_all | solution.py:174
  191.5 142.3 %copy-start.7 = (s32[256]{0:T(256)S(1)}, s32[256]{0:T(256)}, u32[]{:S(2)}) copy-start(s32[256]{0:T(256)} %ids.3) | copy-start | bytes 3076

commit v3 on v2

v3 whole, which is shorter than its diff:
```python
import jax
import jax.numpy as jnp
from jax import lax
from jax.experimental import pallas as pl
from jax.experimental.pallas import tpu as pltpu
from jax.sharding import PartitionSpec as P

BOTH = ("expert", "replica")
F32, BF16 = jnp.float32, jnp.bfloat16
MIB = 1 << 20


def each(n, body, unroll=1):
    def step(s, carry):
        body(s)
        return carry

    lax.fori_loop(0, n, step, 0, unroll=unroll)


ANY = pl.BlockSpec(memory_space=pl.ANY)


def gather_rows(ids, w_gate, w_up):
    experts, r, width = w_gate.shape
    blocks = ids.shape[0]
    pieces = 8
    share, lot = blocks // pieces, experts // 4

    def body(ids, gate_hbm, up_hbm, out_hbm, gate, up, out, in_sems, out_sems):
        def arrivals():
            for q in range(4):
                at = pl.ds(q * lot, lot)
                yield pltpu.make_async_copy(gate_hbm.at[at], gate.at[at], in_sems.at[q])
                yield pltpu.make_async_copy(up_hbm.at[at], up.at[at], in_sems.at[4 + q])

        for copy in arrivals():
            copy.start()
        for copy in arrivals():
            copy.wait()

        def leave(p):
            at = pl.ds(p * share, share)
            return pltpu.make_async_copy(out.at[at], out_hbm.at[at], out_sems.at[p])

        for p in range(pieces):
            def one(b):
                j = ids[p * share + b]
                out[p * share + b, :, :width] = gate[j]
                out[p * share + b, :, width:] = up[j]

            each(share, one, 8)
            leave(p).start()
        for p in range(pieces):
            leave(p).wait()

    return pl.pallas_call(
        body,
        out_shape=jax.ShapeDtypeStruct((blocks, r, 2 * width), BF16),
        grid_spec=pltpu.PrefetchScalarGridSpec(
            num_scalar_prefetch=1,
            grid=(1,),
            in_specs=[ANY, ANY],
            out_specs=ANY,
            scratch_shapes=[
                pltpu.VMEM((experts, r, width), BF16),
                pltpu.VMEM((experts, r, width), BF16),
                pltpu.VMEM((blocks, r, 2 * width), BF16),
                pltpu.SemaphoreType.DMA((8,)),
                pltpu.SemaphoreType.DMA((pieces,)),
            ],
        ),
        compiler_params=pltpu.CompilerParams(vmem_limit_bytes=60 * MIB),
        name="gather_rows",
    )(ids, w_gate, w_up)


def block_compute(tokens, tokens_t, d_hidden, weights):
    rows, model = tokens.shape
    width = d_hidden.shape[1]
    n = 4
    tile = model // n
    tr, tc = 32, 256

    def body(x_hbm, xt_hbm, dh_hbm, w_hbm, h_hbm, d_hbm, part_hbm, x, xt, dh, w, h, d, part, pre, in_sems, w_sems, out_sems, part_sems):
        def weight(k):
            at = pl.ds(k * tile, tile)
            return pltpu.make_async_copy(w_hbm.at[at], w.at[at], w_sems.at[k])

        get_x = pltpu.make_async_copy(x_hbm, x, in_sems.at[0])
        get_dh = pltpu.make_async_copy(dh_hbm, dh, in_sems.at[1])
        get_xt = pltpu.make_async_copy(xt_hbm, xt, in_sems.at[2])
        get_x.start()
        for k in range(n):
            weight(k).start()
        get_dh.start()
        get_xt.start()
        get_x.wait()
        for k in range(n):
            weight(k).wait()
            at = pl.ds(k * tile, tile)
            term = jnp.dot(x[:, k * tile : (k + 1) * tile], w[at, :], preferred_element_type=F32)
            if k:
                pre[...] += term
            else:
                pre[...] = term
        get_dh.wait()

        @pl.loop(0, rows // tr)
        def _(k):
            at = pl.ds(pl.multiple_of(k * tr, tr), tr)
            for c in range(0, width, tc):
                gate, up = pre[at, c : c + tc], pre[at, width + c : width + c + tc]
                sig = jax.nn.sigmoid(gate)
                act = gate * sig
                g = dh[at, c : c + tc].astype(F32)
                h[at, c : c + tc] = (act * up).astype(BF16)
                d[at, c : c + tc] = (g * up * sig * (1.0 + gate * (1.0 - sig))).astype(BF16)
                d[at, width + c : width + c + tc] = (g * act).astype(BF16)

        put_h = pltpu.make_async_copy(h, h_hbm, out_sems.at[0])
        put_d = pltpu.make_async_copy(d, d_hbm, out_sems.at[1])
        get_xt.wait()

        def term_out(k):
            at = pl.ds(k * tile, tile)
            return pltpu.make_async_copy(part.at[at], part_hbm.at[at], part_sems.at[k])

        for k in range(n):
            at = pl.ds(k * tile, tile)
            part[at, :] = jnp.dot(xt[at, :], d[...], preferred_element_type=F32).astype(BF16)
            term_out(k).start()
        put_h.start()
        put_d.start()
        for k in range(n):
            term_out(k).wait()
        put_h.wait()
        put_d.wait()

    outs = [(rows, width), (rows, 2 * width), (model, 2 * width)]
    return pl.pallas_call(
        body,
        out_shape=[jax.ShapeDtypeStruct(o, BF16) for o in outs],
        in_specs=[ANY] * 4,
        out_specs=[ANY] * 3,
        scratch_shapes=[
            pltpu.VMEM((rows, model), BF16),
            pltpu.VMEM((model, rows), BF16),
            pltpu.VMEM((rows, width), BF16),
            pltpu.VMEM((model, 2 * width), BF16),
            *[pltpu.VMEM(o, BF16) for o in outs],
            pltpu.VMEM((rows, 2 * width), F32),
            pltpu.SemaphoreType.DMA((3,)),
            pltpu.SemaphoreType.DMA((n,)),
            pltpu.SemaphoreType.DMA((2,)),
            pltpu.SemaphoreType.DMA((n,)),
        ],
        compiler_params=pltpu.CompilerParams(vmem_limit_bytes=60 * MIB),
        cost_estimate=pl.CostEstimate(
            flops=8 * rows * model * width, bytes_accessed=20 * MIB, transcendentals=rows * width
        ),
        name="block_compute",
    )(tokens, tokens_t, d_hidden, weights)


def token_gradient(d_both, weights):
    rows, deep = d_both.shape
    model = weights.shape[0]
    tile = min(256, model)

    def body(d, w, out):
        out[...] = lax.dot_general(
            d[...], w[...], (((1,), (1,)), ((), ())), preferred_element_type=F32
        ).astype(BF16)

    return pl.pallas_call(
        body,
        out_shape=jax.ShapeDtypeStruct((rows, model), BF16),
        grid=(model // tile,),
        in_specs=[pl.BlockSpec((rows, deep), lambda i: (0, 0)), pl.BlockSpec((tile, deep), lambda i: (i, 0))],
        out_specs=pl.BlockSpec((rows, tile), lambda i: (0, i)),
        compiler_params=pltpu.CompilerParams(vmem_limit_bytes=60 * MIB),
        cost_estimate=pl.CostEstimate(flops=2 * rows * model * deep, bytes_accessed=10 * MIB, transcendentals=0),
        name="token_gradient",
    )(d_both, weights)


def sum_terms(ids, terms, experts, width, scale):
    blocks, r, _ = terms.shape
    pieces, lots = 8, 4
    share, lot = blocks // pieces, experts // lots

    def body(ids, term_hbm, gate_hbm, up_hbm, term, total, gate, up, in_sems, gate_sems, up_sems):
        def arrive(p):
            at = pl.ds(p * share, share)
            return pltpu.make_async_copy(term_hbm.at[at], term.at[at], in_sems.at[p])

        for p in range(pieces):
            arrive(p).start()
        total[...] = jnp.zeros_like(total)
        for p in range(pieces):
            arrive(p).wait()

            def one(b):
                j = ids[p * share + b]
                total[j] = total[j] + term[p * share + b].astype(F32)

            each(share, one, 4)

        def leave(q):
            at = pl.ds(q * lot, lot)
            return (
                pltpu.make_async_copy(gate.at[at], gate_hbm.at[at], gate_sems.at[q]),
                pltpu.make_async_copy(up.at[at], up_hbm.at[at], up_sems.at[q]),
            )

        for q in range(lots):
            def out(j):
                gate[q * lot + j] = (total[q * lot + j, :, :width] * scale).astype(BF16)
                up[q * lot + j] = (total[q * lot + j, :, width:] * scale).astype(BF16)

            each(lot, out, 4)
            for copy in leave(q):
                copy.start()
        for q in range(lots):
            for copy in leave(q):
                copy.wait()

    return pl.pallas_call(
        body,
        out_shape=[jax.ShapeDtypeStruct((experts, r, width), BF16)] * 2,
        grid_spec=pltpu.PrefetchScalarGridSpec(
            num_scalar_prefetch=1,
            grid=(1,),
            in_specs=[ANY],
            out_specs=[ANY] * 2,
            scratch_shapes=[
                pltpu.VMEM((blocks, r, 2 * width), BF16),
                pltpu.VMEM((experts, r, 2 * width), F32),
                pltpu.VMEM((experts, r, width), BF16),
                pltpu.VMEM((experts, r, width), BF16),
                pltpu.SemaphoreType.DMA((pieces,)),
                pltpu.SemaphoreType.DMA((lots,)),
                pltpu.SemaphoreType.DMA((lots,)),
            ],
        ),
        compiler_params=pltpu.CompilerParams(vmem_limit_bytes=60 * MIB),
        name="sum_terms",
    )(ids, terms)


def exchange(parts):
    return lax.all_to_all(parts, BOTH, split_axis=0, concat_axis=0, tiled=True)


def per_device(tokens, d_hidden, w_gate, w_up, expert_ids):
    experts, r, width = w_gate.shape
    blocks = expert_ids.shape[0]
    model = blocks * r
    weights = exchange(gather_rows(expert_ids, w_gate, w_up)).reshape(model, 2 * width)
    tokens_t = lax.optimization_barrier(tokens.T)
    hidden, d_both, part = block_compute(tokens, tokens_t, d_hidden, weights)
    terms = exchange(part.reshape(blocks, r, 2 * width))
    token_grad = token_gradient(d_both, weights)
    grad_gate, grad_up = sum_terms(expert_ids, terms, experts, width, tokens.shape[0] ** (-0.5))
    return hidden, token_grad, grad_gate, grad_up


def solution(mesh):
    rows, weights = P(BOTH, None), P(None, BOTH, None)
    return jax.shard_map(
        per_device,
        mesh=mesh,
        in_specs=(rows, rows, weights, weights, P()),
        out_specs=(rows, rows, weights, weights),
        check_vma=False,
    )
```

time: 342 us -> 332 us (0.971)
  local copies, waits for them, and re-layouts: 14 us -> 2.51 us
    unnamed x23 -> x3, local copies, waits for them, and re-layouts: 14 us -> 2.51 us
    pallas_call x1, Pallas kernels: 1.42 us -> 5.36 us  [gather_rows(): pl.pallas_call(body, out_shape=jax.ShapeDtypeStruct((blocks, r, 2 * width...]
where the time goes in v3:
time: 332 us; the launch traced here: 331 us
  waiting for transfers between devices  273 us (82%)
  Pallas kernels  31.6 us (10%)
  starting transfers between devices  23.8 us (7%)
    all_to_all x2, waiting for transfers between devices, exchange(): return lax.all_to_all(parts, BOTH, split_axis=0, concat_axis=0, tiled=True)  273 us
    all_to_all x2, starting transfers between devices, exchange(): return lax.all_to_all(parts, BOTH, split_axis=0, concat_axis=0, tiled=True)  23.8 us
    pallas_call x1, Pallas kernels, block_compute(): pl.pallas_call(body, out_shape=[jax.ShapeDtypeStruct(o, BF16) for o in ou...  11.3 us
    pallas_call x1, Pallas kernels, token_gradient(): pl.pallas_call(body, out_shape=jax.ShapeDtypeStruct((rows, model), BF16),...  9.32 us
  transfers between devices with their start and end apart: 2, of which 2 were waited for; matrix products, arithmetic and copies ran while one was open for 1% of the time, Pallas kernels for 3%

profile of v3, /device:TPU:1, one launch (start us, length us, event | category | flops | bytes accessed | tf_op | source)
XLA Modules:
  0.0 331.4 jit_solution(6954259636906986272)
XLA Ops:
  0.6 5.4 %gather_rows.1 = bf16[256,8,1536]{2,1,0:T(8,128)(2,1)} custom-call(s32[256]{0:T(256)} %ids.3, bf16[128,8,768]{2,1,0:T(8,128)(2,1)} %gate_hbm.1, bf16[128,8,768]{2,1,0:T(8,128)(2,1)} %up_hbm.1), custom_call_target="tpu_custom_call" | custom-call | tf_op jit(solution)/shard_map/gather_rows/pallas_call | solution.py:57
  6.0 0.0 copy-start
  6.0 16.5 %all-to-all-start = ((bf16[256,8,1536]{2,1,0:T(8,128)(2,1)}), bf16[256,8,1536]{2,1,0:T(8,128)(2,1)}, u32[]{:S(2)}, u32[]{:S(2)}) async-start(bf16[256,8,1536]{2,1,0:T(8,128)(2,1)} %gather_rows.1), calls=%async_computation | async-start | bytes 12582912 | tf_op jit(solution)/shard_map/all_to_all | solution.py:253
  22.6 0.0 copy-done
  22.6 2.5 copy.9
  25.1 139.8 %all-to-all-done = bf16[256,8,1536]{2,1,0:T(8,128)(2,1)} async-done(((bf16[256,8,1536]{2,1,0:T(8,128)(2,1)}), bf16[256,8,1536]{2,1,0:T(8,128)(2,1)}, u32[]{:S(2)}, u32[]{:S(2)}) %all-to-all-start) | async-done | bytes 6291488 | tf_op jit(solution)/shard_map/all_to_all | solution.py:253
  164.8 11.3 %block_compute.1 = (bf16[512,768]{1,0:T(8,128)(2,1)}, bf16[512,1536]{1,0:T(8,128)(2,1)}, bf16[2048,1536]{1,0:T(8,128)(2,1)}) custom-call(bf16[512,2048]{1,0:T(8,128)(2,1)} %x_hbm.1, bf16[2048,512]{1,0:T(8,128)(2,1)} %bitcast.4, bf16[512,768]{1,0:T(8,128)(2,1)} %dh_hbm.1, bf16[2048,1536]{1,0:T(8,128)(2,1)} %bitcast.1.w_hbm.w), custom_call_target="tpu_custom_call" | custom-call | flops 6442450944 | bytes 20971520 | tf_op jit(solution)/shard_map/block_compute/pallas_call | solution.py:141
  176.2 7.3 %all-to-all-start.1 = ((bf16[256,8,1536]{2,1,0:T(8,128)(2,1)}), bf16[256,8,1536]{2,1,0:T(8,128)(2,1)}, u32[]{:S(2)}, u32[]{:S(2)}) async-start(bf16[256,8,1536]{2,1,0:T(8,128)(2,1)} %bitcast.3), calls=%async_computation.1 | async-start | bytes 12582912 | tf_op jit(solution)/shard_map/all_to_all | solution.py:253
  183.5 9.3 %token_gradient.1 = bf16[512,2048]{1,0:T(8,128)(2,1)} custom-call(bf16[512,1536]{1,0:T(8,128)(2,1)} %get-tuple-element.10.d, bf16[2048,1536]{1,0:T(8,128)(2,1)} %bitcast.1.w_hbm.w), custom_call_target="tpu_custom_call" | custom-call | flops 3221225472 | bytes 10485760 | tf_op jit(solution)/shard_map/token_gradient/pallas_call | solution.py:176
  192.8 132.9 %all-to-all-done.1.term_hbm = bf16[256,8,1536]{2,1,0:T(8,128)(2,1)} async-done(((bf16[256,8,1536]{2,1,0:T(8,128)(2,1)}), bf16[256,8,1536]{2,1,0:T(8,128)(2,1)}, u32[]{:S(2)}, u32[]{:S(2)}) %all-to-all-start.1) | async-done | bytes 6291488 | tf_op jit(solution)/shard_map/all_to_all | solution.py:253
  325.8 5.6 %sum_terms.1 = (bf16[128,8,768]{2,1,0:T(8,128)(2,1)}, bf16[128,8,768]{2,1,0:T(8,128)(2,1)}) custom-call(s32[256]{0:T(256)} %ids.3, bf16[256,8,1536]{2,1,0:T(8,128)(2,1)} %all-to-all-done.1.term_hbm), custom_call_target="tpu_custom_call" | custom-call | tf_op jit(solution)/shard_map/sum_terms/pallas_call | solution.py:229
Async XLA Ops:
  6.0 16.6 %copy-start = (bf16[512,2048]{1,0:T(8,128)(2,1)S(1)}, bf16[512,2048]{1,0:T(8,128)(2,1)}, u32[]{:S(2)}) copy-start(bf16[512,2048]{1,0:T(8,128)(2,1)} %x_hbm.1) | copy-start | bytes 6291460
  6.0 158.8 %all-to-all-start = ((bf16[256,8,1536]{2,1,0:T(8,128)(2,1)}), bf16[256,8,1536]{2,1,0:T(8,128)(2,1)}, u32[]{:S(2)}, u32[]{:S(2)}) async-start(bf16[256,8,1536]{2,1,0:T(8,128)(2,1)} %gather_rows.1), calls=%async_computation | async-start | bytes 12582912 | tf_op jit(solution)/shard_map/all_to_all | solution.py:253
  176.2 149.6 %all-to-all-start.1 = ((bf16[256,8,1536]{2,1,0:T(8,128)(2,1)}), bf16[256,8,1536]{2,1,0:T(8,128)(2,1)}, u32[]{:S(2)}, u32[]{:S(2)}) async-start(bf16[256,8,1536]{2,1,0:T(8,128)(2,1)} %bitcast.3), calls=%async_computation.1 | async-start | bytes 12582912 | tf_op jit(solution)/shard_map/all_to_all | solution.py:253

commit v4 on v3

--- a/solution.py
+++ b/solution.py
@@ -28,16 +28,23 @@
     share, lot = blocks // pieces, experts // 4
 
     def body(ids, gate_hbm, up_hbm, out_hbm, gate, up, out, in_sems, out_sems):
-        def arrivals():
-            for q in range(4):
-                at = pl.ds(q * lot, lot)
-                yield pltpu.make_async_copy(gate_hbm.at[at], gate.at[at], in_sems.at[q])
-                yield pltpu.make_async_copy(up_hbm.at[at], up.at[at], in_sems.at[4 + q])
-
-        for copy in arrivals():
-            copy.start()
-        for copy in arrivals():
-            copy.wait()
+        def arrival(source, target, first, q):
+            at = pl.ds(q * lot, lot)
+            return pltpu.make_async_copy(source.at[at], target.at[at], in_sems.at[first + q])
+
+        for q in range(4):
+            arrival(gate_hbm, gate, 0, q).start()
+        for q in range(4):
+            arrival(up_hbm, up, 4, q).start()
+        for q in range(4):
+            arrival(gate_hbm, gate, 0, q).wait()
+
+        def gate_half(b):
+            out[b, :, :width] = gate[ids[b]]
+
+        each(blocks, gate_half, 8)
+        for q in range(4):
+            arrival(up_hbm, up, 4, q).wait()
 
         def leave(p):
             at = pl.ds(p * share, share)
@@ -45,9 +52,7 @@
 
         for p in range(pieces):
             def one(b):
-                j = ids[p * share + b]
-                out[p * share + b, :, :width] = gate[j]
-                out[p * share + b, :, width:] = up[j]
+                out[p * share + b, :, width:] = up[ids[p * share + b]]
 
             each(share, one, 8)
             leave(p).start()
@@ -78,25 +83,28 @@
 def block_compute(tokens, tokens_t, d_hidden, weights):
     rows, model = tokens.shape
     width = d_hidden.shape[1]
-    n = 4
-    tile = model // n
+    n, pieces = 4, 8
+    tile, piece = model // n, model // pieces
     tr, tc = 32, 256
 
-    def body(x_hbm, xt_hbm, dh_hbm, w_hbm, h_hbm, d_hbm, part_hbm, x, xt, dh, w, h, d, part, pre, in_sems, w_sems, out_sems, part_sems):
+    def body(x_hbm, xt_hbm, dh_hbm, w_hbm, h_hbm, d_hbm, part_hbm, x, xt, dh, w, h, d, part, pre, in_sems, x_sems, w_sems, out_sems, part_sems):
         def weight(k):
             at = pl.ds(k * tile, tile)
             return pltpu.make_async_copy(w_hbm.at[at], w.at[at], w_sems.at[k])
 
-        get_x = pltpu.make_async_copy(x_hbm, x, in_sems.at[0])
-        get_dh = pltpu.make_async_copy(dh_hbm, dh, in_sems.at[1])
-        get_xt = pltpu.make_async_copy(xt_hbm, xt, in_sems.at[2])
-        get_x.start()
+        def columns(k):
+            at = pl.ds(k * tile, tile)
+            return pltpu.make_async_copy(x_hbm.at[:, at], x.at[:, at], x_sems.at[k])
+
+        get_dh = pltpu.make_async_copy(dh_hbm, dh, in_sems.at[0])
+        get_xt = pltpu.make_async_copy(xt_hbm, xt, in_sems.at[1])
         for k in range(n):
+            columns(k).start()
             weight(k).start()
         get_dh.start()
         get_xt.start()
-        get_x.wait()
         for k in range(n):
+            columns(k).wait()
             weight(k).wait()
             at = pl.ds(k * tile, tile)
             term = jnp.dot(x[:, k * tile : (k + 1) * tile], w[at, :], preferred_element_type=F32)
@@ -120,19 +128,19 @@
 
         put_h = pltpu.make_async_copy(h, h_hbm, out_sems.at[0])
         put_d = pltpu.make_async_copy(d, d_hbm, out_sems.at[1])
+        put_h.start()
+        put_d.start()
         get_xt.wait()
 
         def term_out(k):
-            at = pl.ds(k * tile, tile)
+            at = pl.ds(k * piece, piece)
             return pltpu.make_async_copy(part.at[at], part_hbm.at[at], part_sems.at[k])
 
-        for k in range(n):
-            at = pl.ds(k * tile, tile)
+        for k in range(pieces):
+            at = pl.ds(k * piece, piece)
             part[at, :] = jnp.dot(xt[at, :], d[...], preferred_element_type=F32).astype(BF16)
             term_out(k).start()
-        put_h.start()
-        put_d.start()
-        for k in range(n):
+        for k in range(pieces):
             term_out(k).wait()
         put_h.wait()
         put_d.wait()
@@ -150,10 +158,11 @@
             pltpu.VMEM((model, 2 * width), BF16),
             *[pltpu.VMEM(o, BF16) for o in outs],
             pltpu.VMEM((rows, 2 * width), F32),
-            pltpu.SemaphoreType.DMA((3,)),
+            pltpu.SemaphoreType.DMA((2,)),
+            pltpu.SemaphoreType.DMA((n,)),
             pltpu.SemaphoreType.DMA((n,)),
             pltpu.SemaphoreType.DMA((2,)),
-            pltpu.SemaphoreType.DMA((n,)),
+            pltpu.SemaphoreType.DMA((pieces,)),
         ],
         compiler_params=pltpu.CompilerParams(vmem_limit_bytes=60 * MIB),
         cost_estimate=pl.CostEstimate(

time: 332 us -> 331 us (level)
  no operation moved by 1% of the time
where the time goes in v4:
time: 331 us
  waiting for transfers between devices  273 us (82%)
  Pallas kernels  30.9 us (9%)
  starting transfers between devices  23.8 us (7%)
    all_to_all x2, waiting for transfers between devices, exchange(): return lax.all_to_all(parts, BOTH, split_axis=0, concat_axis=0, tiled=True)  273 us
    all_to_all x2, starting transfers between devices, exchange(): return lax.all_to_all(parts, BOTH, split_axis=0, concat_axis=0, tiled=True)  23.8 us
    pallas_call x1, Pallas kernels, block_compute(): pl.pallas_call(body, out_shape=[jax.ShapeDtypeStruct(o, BF16) for o in ou...  10.6 us
    pallas_call x1, Pallas kernels, token_gradient(): pl.pallas_call(body, out_shape=jax.ShapeDtypeStruct((rows, model), BF16),...  9.34 us
  transfers between devices with their start and end apart: 2, of which 2 were waited for; matrix products, arithmetic and copies ran while one was open for 1% of the time, Pallas kernels for 3%

profile of v4, /device:TPU:1, one launch (start us, length us, event | category | flops | bytes accessed | tf_op | source)
XLA Modules:
  0.0 330.7 jit_solution(17938982300387588198)
XLA Ops:
  0.6 5.3 %gather_rows.1 = bf16[256,8,1536]{2,1,0:T(8,128)(2,1)} custom-call(s32[256]{0:T(256)} %ids.3, bf16[128,8,768]{2,1,0:T(8,128)(2,1)} %gate_hbm.1, bf16[128,8,768]{2,1,0:T(8,128)(2,1)} %up_hbm.1), custom_call_target="tpu_custom_call" | custom-call | tf_op jit(solution)/shard_map/gather_rows/pallas_call | solution.py:62
  6.0 0.0 copy-start
  6.0 16.5 %all-to-all-start = ((bf16[256,8,1536]{2,1,0:T(8,128)(2,1)}), bf16[256,8,1536]{2,1,0:T(8,128)(2,1)}, u32[]{:S(2)}, u32[]{:S(2)}) async-start(bf16[256,8,1536]{2,1,0:T(8,128)(2,1)} %gather_rows.1), calls=%async_computation | async-start | bytes 12582912 | tf_op jit(solution)/shard_map/all_to_all | solution.py:262
  22.5 0.0 copy-done
  22.5 2.5 copy.9
  25.0 139.8 %all-to-all-done = bf16[256,8,1536]{2,1,0:T(8,128)(2,1)} async-done(((bf16[256,8,1536]{2,1,0:T(8,128)(2,1)}), bf16[256,8,1536]{2,1,0:T(8,128)(2,1)}, u32[]{:S(2)}, u32[]{:S(2)}) %all-to-all-start) | async-done | bytes 6291488 | tf_op jit(solution)/shard_map/all_to_all | solution.py:262
  164.8 10.6 %block_compute.1 = (bf16[512,768]{1,0:T(8,128)(2,1)}, bf16[512,1536]{1,0:T(8,128)(2,1)}, bf16[2048,1536]{1,0:T(8,128)(2,1)}) custom-call(bf16[512,2048]{1,0:T(8,128)(2,1)} %x_hbm.1, bf16[2048,512]{1,0:T(8,128)(2,1)} %bitcast.4, bf16[512,768]{1,0:T(8,128)(2,1)} %dh_hbm.1, bf16[2048,1536]{1,0:T(8,128)(2,1)} %bitcast.1.w_hbm.w), custom_call_target="tpu_custom_call" | custom-call | flops 6442450944 | bytes 20971520 | tf_op jit(solution)/shard_map/block_compute/pallas_call | solution.py:149
  175.4 7.3 %all-to-all-start.1 = ((bf16[256,8,1536]{2,1,0:T(8,128)(2,1)}), bf16[256,8,1536]{2,1,0:T(8,128)(2,1)}, u32[]{:S(2)}, u32[]{:S(2)}) async-start(bf16[256,8,1536]{2,1,0:T(8,128)(2,1)} %bitcast.3), calls=%async_computation.1 | async-start | bytes 12582912 | tf_op jit(solution)/shard_map/all_to_all | solution.py:262
  182.8 9.3 %token_gradient.1 = bf16[512,2048]{1,0:T(8,128)(2,1)} custom-call(bf16[512,1536]{1,0:T(8,128)(2,1)} %get-tuple-element.10.d, bf16[2048,1536]{1,0:T(8,128)(2,1)} %bitcast.1.w_hbm.w), custom_call_target="tpu_custom_call" | custom-call | flops 3221225472 | bytes 10485760 | tf_op jit(solution)/shard_map/token_gradient/pallas_call | solution.py:185
  192.1 132.9 %all-to-all-done.1.term_hbm = bf16[256,8,1536]{2,1,0:T(8,128)(2,1)} async-done(((bf16[256,8,1536]{2,1,0:T(8,128)(2,1)}), bf16[256,8,1536]{2,1,0:T(8,128)(2,1)}, u32[]{:S(2)}, u32[]{:S(2)}) %all-to-all-start.1) | async-done | bytes 6291488 | tf_op jit(solution)/shard_map/all_to_all | solution.py:262
  325.0 5.6 %sum_terms.1 = (bf16[128,8,768]{2,1,0:T(8,128)(2,1)}, bf16[128,8,768]{2,1,0:T(8,128)(2,1)}) custom-call(s32[256]{0:T(256)} %ids.3, bf16[256,8,1536]{2,1,0:T(8,128)(2,1)} %all-to-all-done.1.term_hbm), custom_call_target="tpu_custom_call" | custom-call | tf_op jit(solution)/shard_map/sum_terms/pallas_call | solution.py:238
Async XLA Ops:
  6.0 16.6 %copy-start = (bf16[512,2048]{1,0:T(8,128)(2,1)S(1)}, bf16[512,2048]{1,0:T(8,128)(2,1)}, u32[]{:S(2)}) copy-start(bf16[512,2048]{1,0:T(8,128)(2,1)} %x_hbm.1) | copy-start | bytes 6291460
  6.0 158.8 %all-to-all-start = ((bf16[256,8,1536]{2,1,0:T(8,128)(2,1)}), bf16[256,8,1536]{2,1,0:T(8,128)(2,1)}, u32[]{:S(2)}, u32[]{:S(2)}) async-start(bf16[256,8,1536]{2,1,0:T(8,128)(2,1)} %gather_rows.1), calls=%async_computation | async-start | bytes 12582912 | tf_op jit(solution)/shard_map/all_to_all | solution.py:262
  175.4 149.6 %all-to-all-start.1 = ((bf16[256,8,1536]{2,1,0:T(8,128)(2,1)}), bf16[256,8,1536]{2,1,0:T(8,128)(2,1)}, u32[]{:S(2)}, u32[]{:S(2)}) async-start(bf16[256,8,1536]{2,1,0:T(8,128)(2,1)} %bitcast.3), calls=%async_computation.1 | async-start | bytes 12582912 | tf_op jit(solution)/shard_map/all_to_all | solution.py:262

commit v5 on v4

--- a/solution.py
+++ b/solution.py
@@ -199,7 +199,7 @@
     pieces, lots = 8, 4
     share, lot = blocks // pieces, experts // lots
 
-    def body(ids, term_hbm, gate_hbm, up_hbm, term, total, gate, up, in_sems, gate_sems, up_sems):
+    def body(ids, term_hbm, gate_hbm, up_hbm, term, total, other, gate, up, in_sems, gate_sems, up_sems):
         def arrive(p):
             at = pl.ds(p * share, share)
             return pltpu.make_async_copy(term_hbm.at[at], term.at[at], in_sems.at[p])
@@ -207,14 +207,19 @@
         for p in range(pieces):
             arrive(p).start()
         total[...] = jnp.zeros_like(total)
+        other[...] = jnp.zeros_like(other)
         for p in range(pieces):
             arrive(p).wait()
 
             def one(b):
-                j = ids[p * share + b]
-                total[j] = total[j] + term[p * share + b].astype(F32)
-
-            each(share, one, 4)
+                even = p * share + 2 * b
+                j, k = ids[even], ids[even + 1]
+                first = total[j] + term[even].astype(F32)
+                second = other[k] + term[even + 1].astype(F32)
+                total[j] = first
+                other[k] = second
+
+            each(share // 2, one, 4)
 
         def leave(q):
             at = pl.ds(q * lot, lot)
@@ -225,8 +230,9 @@
 
         for q in range(lots):
             def out(j):
-                gate[q * lot + j] = (total[q * lot + j, :, :width] * scale).astype(BF16)
-                up[q * lot + j] = (total[q * lot + j, :, width:] * scale).astype(BF16)
+                grad = (total[q * lot + j] + other[q * lot + j]) * scale
+                gate[q * lot + j] = grad[:, :width].astype(BF16)
+                up[q * lot + j] = grad[:, width:].astype(BF16)
 
             each(lot, out, 4)
             for copy in leave(q):
@@ -245,6 +251,7 @@
             out_specs=[ANY] * 2,
             scratch_shapes=[
                 pltpu.VMEM((blocks, r, 2 * width), BF16),
+                pltpu.VMEM((experts, r, 2 * width), F32),
                 pltpu.VMEM((experts, r, 2 * width), F32),
                 pltpu.VMEM((experts, r, width), BF16),
                 pltpu.VMEM((experts, r, width), BF16),

time: 331 us -> 331 us (level)
  no operation moved by 1% of the time
where the time goes in v5:
time: 331 us
  waiting for transfers between devices  273 us (82%)
  Pallas kernels  30.9 us (9%)
  starting transfers between devices  23.8 us (7%)
    all_to_all x2, waiting for transfers between devices, exchange(): return lax.all_to_all(parts, BOTH, split_axis=0, concat_axis=0, tiled=True)  273 us
    all_to_all x2, starting transfers between devices, exchange(): return lax.all_to_all(parts, BOTH, split_axis=0, concat_axis=0, tiled=True)  23.8 us
    pallas_call x1, Pallas kernels, block_compute(): pl.pallas_call(body, out_shape=[jax.ShapeDtypeStruct(o, BF16) for o in ou...  10.6 us
    pallas_call x1, Pallas kernels, token_gradient(): pl.pallas_call(body, out_shape=jax.ShapeDtypeStruct((rows, model), BF16),...  9.34 us
  transfers between devices with their start and end apart: 2, of which 2 were waited for; matrix products, arithmetic and copies ran while one was open for 1% of the time, Pallas kernels for 3%

profile of v5, /device:TPU:1, one launch (start us, length us, event | category | flops | bytes accessed | tf_op | source)
XLA Modules:
  0.0 330.7 jit_solution(13850299153385844555)
XLA Ops:
  0.6 5.3 %gather_rows.1 = bf16[256,8,1536]{2,1,0:T(8,128)(2,1)} custom-call(s32[256]{0:T(256)} %ids.3, bf16[128,8,768]{2,1,0:T(8,128)(2,1)} %gate_hbm.1, bf16[128,8,768]{2,1,0:T(8,128)(2,1)} %up_hbm.1), custom_call_target="tpu_custom_call" | custom-call | tf_op jit(solution)/shard_map/gather_rows/pallas_call | solution.py:62
  6.0 0.0 copy-start
  6.0 16.5 %all-to-all-start = ((bf16[256,8,1536]{2,1,0:T(8,128)(2,1)}), bf16[256,8,1536]{2,1,0:T(8,128)(2,1)}, u32[]{:S(2)}, u32[]{:S(2)}) async-start(bf16[256,8,1536]{2,1,0:T(8,128)(2,1)} %gather_rows.1), calls=%async_computation | async-start | bytes 12582912 | tf_op jit(solution)/shard_map/all_to_all | solution.py:269
  22.5 0.0 copy-done
  22.5 2.5 copy.9
  25.0 139.8 %all-to-all-done = bf16[256,8,1536]{2,1,0:T(8,128)(2,1)} async-done(((bf16[256,8,1536]{2,1,0:T(8,128)(2,1)}), bf16[256,8,1536]{2,1,0:T(8,128)(2,1)}, u32[]{:S(2)}, u32[]{:S(2)}) %all-to-all-start) | async-done | bytes 6291488 | tf_op jit(solution)/shard_map/all_to_all | solution.py:269
  164.8 10.6 %block_compute.1 = (bf16[512,768]{1,0:T(8,128)(2,1)}, bf16[512,1536]{1,0:T(8,128)(2,1)}, bf16[2048,1536]{1,0:T(8,128)(2,1)}) custom-call(bf16[512,2048]{1,0:T(8,128)(2,1)} %x_hbm.1, bf16[2048,512]{1,0:T(8,128)(2,1)} %bitcast.4, bf16[512,768]{1,0:T(8,128)(2,1)} %dh_hbm.1, bf16[2048,1536]{1,0:T(8,128)(2,1)} %bitcast.1.w_hbm.w), custom_call_target="tpu_custom_call" | custom-call | flops 6442450944 | bytes 20971520 | tf_op jit(solution)/shard_map/block_compute/pallas_call | solution.py:149
  175.4 7.3 %all-to-all-start.1 = ((bf16[256,8,1536]{2,1,0:T(8,128)(2,1)}), bf16[256,8,1536]{2,1,0:T(8,128)(2,1)}, u32[]{:S(2)}, u32[]{:S(2)}) async-start(bf16[256,8,1536]{2,1,0:T(8,128)(2,1)} %bitcast.3), calls=%async_computation.1 | async-start | bytes 12582912 | tf_op jit(solution)/shard_map/all_to_all | solution.py:269
  182.8 9.3 %token_gradient.1 = bf16[512,2048]{1,0:T(8,128)(2,1)} custom-call(bf16[512,1536]{1,0:T(8,128)(2,1)} %get-tuple-element.10.d, bf16[2048,1536]{1,0:T(8,128)(2,1)} %bitcast.1.w_hbm.w), custom_call_target="tpu_custom_call" | custom-call | flops 3221225472 | bytes 10485760 | tf_op jit(solution)/shard_map/token_gradient/pallas_call | solution.py:185
  192.1 132.9 %all-to-all-done.1.term_hbm = bf16[256,8,1536]{2,1,0:T(8,128)(2,1)} async-done(((bf16[256,8,1536]{2,1,0:T(8,128)(2,1)}), bf16[256,8,1536]{2,1,0:T(8,128)(2,1)}, u32[]{:S(2)}, u32[]{:S(2)}) %all-to-all-start.1) | async-done | bytes 6291488 | tf_op jit(solution)/shard_map/all_to_all | solution.py:269
  325.0 5.6 %sum_terms.1 = (bf16[128,8,768]{2,1,0:T(8,128)(2,1)}, bf16[128,8,768]{2,1,0:T(8,128)(2,1)}) custom-call(s32[256]{0:T(256)} %ids.3, bf16[256,8,1536]{2,1,0:T(8,128)(2,1)} %all-to-all-done.1.term_hbm), custom_call_target="tpu_custom_call" | custom-call | tf_op jit(solution)/shard_map/sum_terms/pallas_call | solution.py:244
Async XLA Ops:
  6.0 16.6 %copy-start = (bf16[512,2048]{1,0:T(8,128)(2,1)S(1)}, bf16[512,2048]{1,0:T(8,128)(2,1)}, u32[]{:S(2)}) copy-start(bf16[512,2048]{1,0:T(8,128)(2,1)} %x_hbm.1) | copy-start | bytes 6291460
  6.0 158.8 %all-to-all-start = ((bf16[256,8,1536]{2,1,0:T(8,128)(2,1)}), bf16[256,8,1536]{2,1,0:T(8,128)(2,1)}, u32[]{:S(2)}, u32[]{:S(2)}) async-start(bf16[256,8,1536]{2,1,0:T(8,128)(2,1)} %gather_rows.1), calls=%async_computation | async-start | bytes 12582912 | tf_op jit(solution)/shard_map/all_to_all | solution.py:269
  175.4 149.6 %all-to-all-start.1 = ((bf16[256,8,1536]{2,1,0:T(8,128)(2,1)}), bf16[256,8,1536]{2,1,0:T(8,128)(2,1)}, u32[]{:S(2)}, u32[]{:S(2)}) async-start(bf16[256,8,1536]{2,1,0:T(8,128)(2,1)} %bitcast.3), calls=%async_computation.1 | async-start | bytes 12582912 | tf_op jit(solution)/shard_map/all_to_all | solution.py:269
